TPU v7x, 32 devices: a whole 2x2x4 slice. The times are simulated.
32 devices in a mesh: space: 8 (over y, x, core), snap: 4 (over z).
Axes of the slice: x: 2, y: 2, z: 4, core: 2. Of those that a mesh axis runs over, the one named last changes fastest.
Arguments:
- snapshots: float32 [32768, 512], P('space', 'snap')
- picks: int32 [2, 128], replicated, may hold values from 0 to 511, as said below
Outputs:
- residual: float32 [32768, 512], P('space', 'snap')
- basis_scaled: float32 [32768, 256], P('space')
Inputs may be any that keep to these rules, and one draw needn't show every extreme that they name: All entries of picks are distinct over both dimensions.
All inputs are finite; a program needn't handle non-finite values.
Results may differ from a plain program's by a relative error of at most 0.0003.
Values sent between devices are 32-bit elements; how exact they have to be, the bound alone decides.
A program may use at most 64 MiB of HBM per device.

v0:
```python
import math

import jax
import jax.numpy as jnp
from jax import lax
from jax.sharding import PartitionSpec as P


def hdot(left, right):
    return jnp.dot(left, right, precision=lax.Precision.HIGHEST, preferred_element_type=jnp.float32)


def tdot(left, right):
    return lax.dot_general(
        left,
        right,
        (((0,), (0,)), ((), ())),
        precision=lax.Precision.HIGHEST,
        preferred_element_type=jnp.float32,
    )


def select_table(count, wanted):
    position = jnp.arange(count, dtype=jnp.int32)[:, None]
    return (position == wanted[None, :]).astype(jnp.float32)


def fetch_panel(snapshots, wanted):
    piece = lax.all_gather(snapshots, "snap", axis=1, tiled=True)
    return hdot(piece, select_table(piece.shape[1], wanted))


def gram_sum(panel):
    return lax.psum(tdot(panel, panel), "space")


def on_device(snapshots, picks):
    rows = snapshots.shape[0]
    scale = math.sqrt(rows * lax.axis_size("space"))
    residual = snapshots
    basis = None
    for step in range(picks.shape[0]):
        panel = fetch_panel(snapshots, picks[step])
        if basis is None:
            gram = gram_sum(panel)
        else:
            coef, square = lax.psum((tdot(basis, panel), tdot(panel, panel)), "space")
            panel = panel - hdot(basis, coef)
            gram = square - tdot(coef, coef)
        lower = jnp.linalg.cholesky(gram)
        fresh = jax.scipy.linalg.solve_triangular(lower, panel.T, lower=True).T
        weights = lax.psum(tdot(fresh, residual), "space")
        residual = residual - hdot(fresh, weights)
        basis = fresh if basis is None else jnp.concatenate([basis, fresh], axis=1)
    return (residual, basis * scale)


def solution(mesh):
    placed = (P("space", "snap"), P())
    return jax.shard_map(
        on_device,
        mesh=mesh,
        in_specs=placed,
        out_specs=(P("space", "snap"), P("space", None)),
        check_vma=False,
    )
```

profile of v0, /device:TPU:0, one launch (start us, length us, event | category | flops | bytes accessed | tf_op | source)
XLA Modules:
  0.0 426.9 jit_solution(11672250414879343284)
XLA Ops:
  7.2 0.0 copy-start.11
  7.2 0.0 all-gather.2.cloned.1.call-start
  7.2 0.7 all-gather.2.cloned.1.call-update
  7.9 0.0 all-reduce.5.cloned.1.call-start
  8.0 0.0 copy-done.11
  8.0 153.5 %all-gather.2.cloned.1.call-done = f32[4096,512]{1,0:T(8,128)} async-done(((f32[4096,128]{1,0:T(8,128)}), f32[4096,512]{1,0:T(8,128)}) %all-gather.2.cloned.1.call-update) | async-done | bytes 8388624 | tf_op jit(solution)/shard_map/all_gather | solution.py:29
  161.4 8.1 %fusion.4 = f32[128,4096]{1,0:T(8,128)S(1)} fusion(f32[4096,512]{1,0:T(8,128)} %all-gather.2.cloned.1.call-done, s32[128]{0:T(128)S(1)} %get-tuple-element.10), kind=kOutput, calls=%fused_computation.10 | convolution fusion | flops 3221356544 | bytes 10486272 | tf_op jit(solution)/shard_map/dot_general | solution.py:10
  169.5 0.0 copy-start.2
  169.5 2.4 fusion.16
  171.9 0.0 copy-done.2
  171.9 0.0 all-reduce.5.cloned.1.call-update
  172.0 0.4 all-reduce.9.cloned.1.call-start
  172.4 8.1 %fusion.2 = f32[128,4096]{1,0:T(8,128)S(1)} fusion(f32[4096,512]{1,0:T(8,128)} %all-gather.2.cloned.1.call-done, s32[128]{0:T(128)S(1)} %get-tuple-element.9), kind=kOutput, calls=%fused_computation.9 | convolution fusion | flops 3221356544 | bytes 10486272 | tf_op jit(solution)/shard_map/dot_general | solution.py:10
  180.5 0.0 copy-start
  180.5 2.4 fusion.18
  182.9 39.8 %all-reduce.5.cloned.1.call-done = f32[128,128]{0,1:T(8,128)} async-done(((f32[128,128]{0,1:T(8,128)}), f32[128,128]{0,1:T(8,128)}) %all-reduce.5.cloned.1.call-update) | async-done | bytes 65552 | tf_op jit(solution)/shard_map/psum | solution.py:34
  222.8 0.9 copy.5
  223.7 0.9 fusion.15
  224.6 11.7 %cholesky.44 = f32[128,128]{1,0:T(8,128)S(1)} custom-call(f32[128,128]{1,0:T(8,128)S(1)} %fusion.15), custom_call_target="Cholesky" | custom-call | tf_op jit(solution)/shard_map/jit(cholesky)/cholesky | solution.py:50
  236.3 0.7 compare_reduce_fusion.1
  237.0 0.6 fusion.8
  237.6 9.8 %custom-call.6 = f32[1,128,128]{1,2,0:T(8,128)S(1)} custom-call(f32[1,128,128]{2,1,0:T(8,128)S(1)} %fusion.8), custom_call_target="InvertDiagBlocksLowerTriangular" | custom-call | tf_op jit(solution)/shard_map/jit(_solve_triangular)/triangular_solve | solution.py:51
  247.5 0.0 copy-start.1
  247.5 16.1 %fusion.13 = f32[128,4096]{1,0:T(8,128)S(1)} fusion(f32[128,4096]{1,0:T(8,128)} %copy-done.2, f32[1,128,128]{1,2,0:T(8,128)S(1)} %custom-call.6), kind=kOutput, calls=%fused_computation.21 | convolution fusion | flops 805306368 | bytes 4259840 | tf_op jit(solution)/shard_map/jit(_solve_triangular)/triangular_solve | solution.py:51
  263.6 0.0 copy-start.6
  263.6 2.5 fusion.19
  266.1 2.8 fusion.17
  268.9 0.0 all-reduce.9.cloned.1.call-update
  269.0 0.0 all-reduce.7.cloned.1.call-start
  269.0 53.5 %all-reduce.9.cloned.1.call-done = (f32[128,128]{1,0:T(8,128)}, f32[128,128]{1,0:T(8,128)}, f32[128,128]{0,1:T(8,128)}) async-done(((f32[128,128]{1,0:T(8,128)}, f32[128,128]{1,0:T(8,128)}, f32[128,128]{0,1:T(8,128)}), (f32[128,128]{1,0:T(8,128)}, f32[128,128]{1,0:T(8,128)}, f32[128,128]{0,1:T(8,128)})) %all-reduce.9.cloned.1.call-update) | async-done | bytes 196624 | tf_op jit(solution)/shard_map/psum | solution.py:52
  322.5 4.9 %convolution_subtract_fusion.1 = f32[128,4096]{1,0:T(8,128)} fusion(f32[128,4096]{1,0:T(8,128)} %copy-done, f32[128,128]{1,0:T(8,128)} %get-tuple-element.7, f32[128,4096]{1,0:T(8,128)S(1)} %fusion.13), kind=kOutput, calls=%fused_computation.1 | convolution fusion | flops 805830656 | bytes 6356992 | tf_op jit(solution)/shard_map/dot_general | solution.py:10
  327.4 0.3 convolution_subtract_fusion.3
  327.7 0.1 copy.8
  327.8 11.7 %cholesky.55 = f32[128,128]{1,0:T(8,128)S(1)} custom-call(f32[128,128]{1,0:T(8,128)S(1)} %fusion.12), custom_call_target="Cholesky" | custom-call | tf_op jit(solution)/shard_map/jit(cholesky)/cholesky | solution.py:50
  339.6 0.6 compare_reduce_fusion
  340.2 0.7 fusion.9
  340.9 9.8 %custom-call.7 = f32[1,128,128]{1,2,0:T(8,128)S(1)} custom-call(f32[1,128,128]{2,1,0:T(8,128)S(1)} %fusion.9), custom_call_target="InvertDiagBlocksLowerTriangular" | custom-call | tf_op jit(solution)/shard_map/jit(_solve_triangular)/triangular_solve | solution.py:51
  350.7 0.0 copy-start.7
  350.7 5.3 %convolution_subtract_fusion.2 = f32[4096,128]{1,0:T(8,128)S(1)} fusion(f32[4096,128]{1,0:T(8,128)} %param.5, f32[128,4096]{1,0:T(8,128)S(1)} %fusion.13, f32[128,128]{1,0:T(8,128)S(1)} %copy-done.9), kind=kOutput, calls=%fused_computation.2 | convolution fusion | flops 805830656 | bytes 6356992 | tf_op jit(solution)/shard_map/dot_general | solution.py:10
  356.0 0.0 copy-start.5
  356.0 2.1 fusion.10
  358.2 1.3 copy-done.3
  359.5 2.8 fusion.20
  362.3 0.0 all-reduce.7.cloned.1.call-update
  362.3 4.1 maximum_multiply_fusion
  366.5 5.7 %copy.9 = f32[4096,256]{1,0:T(8,128)} copy(f32[4096,256]{0,1:T(8,128)} %maximum_multiply_fusion) | data formatting | bytes 8388608
  372.2 42.1 %all-reduce.7.cloned.1.call-done = f32[128,128]{1,0:T(8,128)} async-done(((f32[128,128]{1,0:T(8,128)}), f32[128,128]{1,0:T(8,128)}) %all-reduce.7.cloned.1.call-update) | async-done | bytes 65552 | tf_op jit(solution)/shard_map/psum | solution.py:52
  414.3 5.8 %convolution_subtract_fusion = f32[4096,128]{1,0:T(8,128)} fusion(f32[4096,128]{1,0:T(8,128)} %copy-done.5, f32[128,4096]{1,0:T(8,128)S(1)} %copy-done.4, f32[128,128]{1,0:T(8,128)} %all-reduce.7.cloned.1.call-done), kind=kOutput, calls=%fused_computation | convolution fusion | flops 805830656 | bytes 6356992 | tf_op jit(solution)/shard_map/dot_general | solution.py:10
  (18 shorter events, 0.1 us)
Async XLA Ops:
  7.2 0.8 copy-start.11
  7.2 154.3 %all-gather.2.cloned.1.call-start = ((), (), s32[]{:S(2)}) async-start(), calls=%async_computation | async-start | bytes 10485760 | tf_op jit(solution)/shard_map/all_gather | solution.py:29
  7.9 214.9 %all-reduce.5.cloned.1.call-start = ((), (), s32[]{:S(2)}) async-start(), calls=%async_computation.1 | async-start | bytes 131072 | tf_op jit(solution)/shard_map/psum | solution.py:34
  169.5 2.4 copy-start.2
  172.0 150.5 %all-reduce.9.cloned.1.call-start = ((), (), s32[]{:S(2)}) async-start(), calls=%async_computation.3 | async-start | bytes 393216 | tf_op jit(solution)/shard_map/psum | solution.py:52
  180.5 57.1 %copy-start = (f32[128,4096]{1,0:T(8,128)}, f32[128,4096]{1,0:T(8,128)S(1)}, u32[]{:S(2)}) copy-start(f32[128,4096]{1,0:T(8,128)S(1)} %fusion.2) | copy-start | bytes 6291460
  247.5 16.1 %copy-start.1 = (f32[128,4096]{1,0:T(8,128)S(1)}, f32[128,4096]{1,0:T(8,128)}, u32[]{:S(2)}) copy-start(f32[128,4096]{1,0:T(8,128)} %copy-done) | copy-start | bytes 6291460
  263.6 2.5 copy-start.6
  269.0 145.3 %all-reduce.7.cloned.1.call-start = ((), (), s32[]{:S(2)}) async-start(), calls=%async_computation.2 | async-start | bytes 131072 | tf_op jit(solution)/shard_map/psum | solution.py:52
  322.5 4.9 %copy-start.8 = (f32[128,128]{1,0:T(8,128)S(1)}, f32[128,128]{1,0:T(8,128)}, u32[]{:S(2)}) copy-start(f32[128,128]{1,0:T(8,128)} %get-tuple-element.7) | copy-start | bytes 196612
  322.5 4.9 %copy-start.10 = (f32[128,128]{0,1:T(8,128)S(1)}, f32[128,128]{0,1:T(8,128)}, u32[]{:S(2)}) copy-start(f32[128,128]{0,1:T(8,128)} %get-tuple-element.8) | copy-start | bytes 196612
  322.5 28.2 %copy-start.9 = (f32[128,128]{1,0:T(8,128)S(1)}, f32[128,128]{1,0:T(8,128)}, u32[]{:S(2)}) copy-start(f32[128,128]{1,0:T(8,128)} %get-tuple-element.6) | copy-start | bytes 196612
  350.7 5.3 %copy-start.7 = (f32[128,4096]{1,0:T(8,128)S(1)}, f32[128,4096]{1,0:T(8,128)}, u32[]{:S(2)}) copy-start(f32[128,4096]{1,0:T(8,128)} %convolution_subtract_fusion.1) | copy-start | bytes 6291460
  356.0 2.2 copy-start.5
  358.2 1.3 copy-start.3
  366.5 47.8 %copy-start.4 = (f32[128,4096]{1,0:T(8,128)S(1)}, f32[128,4096]{1,0:T(8,128)}, u32[]{:S(2)}) copy-start(f32[128,4096]{1,0:T(8,128)} %copy-done.3) | copy-start | bytes 6291460
Sparse Core Ops, SparseCore 0:
  9.6 151.8 all-gather.1
  172.1 50.6 all-reduce.4
  269.1 53.3 all-reduce.8
  362.5 51.7 all-reduce.6
where the time goes:
time: 426 us; the launch traced here: 427 us
  waiting for transfers between devices  290 us (68%)
  matrix products  63.7 us (15%)
  other arithmetic  50.7 us (12%)
  between operations  14.2 us (3%)
  local copies, waits for them, and re-layouts  8.13 us (2%)
    all_gather x1, waiting for transfers between devices, fetch_panel(): piece = lax.all_gather(snapshots, 'snap', axis=1, tiled=True)  153 us
    psum x2, waiting for transfers between devices, on_device(): weights = lax.psum(tdot(fresh, residual), 'space')  95.5 us
    psum x1, waiting for transfers between devices, gram_sum(): return lax.psum(tdot(panel, panel), 'space')  39.8 us
    dot_general x5, matrix products, hdot(): jnp.dot(left, right, precision=lax.Precision.HIGHEST, preferred_element_t...  32.2 us
    another operation x6, other arithmetic, on_device(): lower = jnp.linalg.cholesky(gram)  24.8 us
    another operation x4, other arithmetic, on_device(): fresh = jax.scipy.linalg.solve_triangular(lower, panel.T, lower=True).T  20.9 us
    another operation x2, matrix products, on_device(): fresh = jax.scipy.linalg.solve_triangular(lower, panel.T, lower=True).T  18.3 us
    dot_general x6, matrix products, tdot(): lax.dot_general(left, right, (((0,), (0,)), ((), ())), precision=lax.Prec...  13.2 us
  transfers between devices with their start and end apart: 4, of which 4 were waited for; matrix products, arithmetic and copies ran while one was open for 5% of the time, Pallas kernels for 0%

commit v1 on v0

v1 whole, which is shorter than its diff:
```python
import functools
import math

import jax
import jax.numpy as jnp
from jax import lax
from jax.experimental import pallas as pl
from jax.experimental.pallas import tpu as pltpu
from jax.sharding import PartitionSpec as P

MESH = pl.DeviceIdType.MESH
HIGHEST = lax.Precision.HIGHEST
LANES = 128


def dot(left, right, contract=((1,), (0,))):
    return lax.dot_general(
        left, right, (contract, ((), ())), precision=HIGHEST, preferred_element_type=jnp.float32
    )


def gather_kernel(
    spaces, snaps, chunk, block,
    x_ref, sel_ref, panel_ref, total_ref,
    own, acc, gram, parts,
    send_sem, recv_sem, gs_sem, gr_sem, bs_sem, br_sem,
):
    me = lax.axis_index("space")
    z = lax.axis_index("snap")
    rows = x_ref.shape[0]
    count = rows // chunk
    lag = min(2, count)
    early = z // (snaps // 2)
    late = 1 - early

    barrier = pltpu.get_barrier_semaphore()
    for k in range(1, spaces):
        pl.semaphore_signal(
            barrier, inc=1, device_id={"space": lax.rem(me + k, spaces)}, device_id_type=MESH
        )
    for k in range(1, snaps):
        pl.semaphore_signal(
            barrier, inc=1, device_id={"snap": lax.rem(z + k, snaps)}, device_id_type=MESH
        )
    pl.semaphore_wait(barrier, spaces + snaps - 2)

    def span(c):
        return pl.ds(pl.multiple_of(c * chunk, chunk), chunk)

    def place(d):
        return z + d * (snaps - 1 - 2 * z)

    def hop(d, c):
        return pltpu.make_async_remote_copy(
            src_ref=acc.at[d, span(c)],
            dst_ref=acc.at[d, span(c)],
            send_sem=send_sem.at[d, c],
            recv_sem=recv_sem.at[d, c],
            device_id={"snap": lax.rem(z + 1 - 2 * d + snaps, snaps)},
            device_id_type=MESH,
        )

    def prepare(c, carry):
        mine = dot(x_ref[span(c), :], sel_ref[...])
        own[span(c), :] = mine

        @pl.when(place(early) == 0)
        def _():
            acc[early, span(c), :] = mine
            hop(early, c).start()

        return carry

    lax.fori_loop(0, count, prepare, 0)
    gram[...] = jnp.zeros_like(gram)

    def relay(c):
        @pl.when(place(early) > 0)
        def _():
            hop(early, c).wait_recv()
            acc[early, span(c), :] = acc[early, span(c), :] + own[span(c), :]
            hop(early, c).start()

    def finish(c):
        hop(late, c).wait_recv()
        panel = acc[late, span(c), :] + acc[early, span(c), :]
        panel_ref[span(c), :] = panel

        @pl.when(place(late) < snaps - 1)
        def _():
            acc[late, span(c), :] = acc[late, span(c), :] + own[span(c), :]
            hop(late, c).start()

        half = panel.shape[1] // 2
        first, second = panel[:, :half], panel[:, half:]
        wide = jnp.concatenate([first, x_ref[span(c), :]], axis=1)
        both = dot(panel, wide, ((0,), (0,)))
        gram[0:2 * half, :] += both[:, :half]
        gram[2 * half:4 * half, :] += both[:, half:]
        gram[4 * half:5 * half, :] += dot(second, second, ((0,), (0,)))

    for c in range(lag):
        relay(c)

    def step(c, carry):
        relay(c)
        finish(c - lag)
        return carry

    lax.fori_loop(lag, count, step, 0)
    for c in range(count - lag, count):
        finish(c)

    def owned(k):
        return pl.ds(pl.multiple_of(k * block, block), block)

    def scatter(k):
        peer = lax.rem(me + k, spaces)
        return pltpu.make_async_remote_copy(
            src_ref=gram.at[owned(peer)],
            dst_ref=parts.at[k],
            send_sem=gs_sem.at[k],
            recv_sem=gr_sem.at[k],
            device_id={"space": peer},
            device_id_type=MESH,
        )

    def spread(k):
        return pltpu.make_async_remote_copy(
            src_ref=total_ref.at[owned(me)],
            dst_ref=total_ref.at[owned(me)],
            send_sem=bs_sem.at[k],
            recv_sem=br_sem.at[k],
            device_id={"space": lax.rem(me + k, spaces)},
            device_id_type=MESH,
        )

    for k in range(1, spaces):
        scatter(k).start()
    mine = gram[owned(me), :]
    for k in range(1, spaces):
        scatter(k).wait_recv()
        mine = mine + parts[k]
    total_ref[owned(me), :] = mine
    for k in range(1, spaces):
        spread(k).start()
    for k in range(1, spaces):
        source = lax.rem(me - k + spaces, spaces)
        pltpu.make_async_remote_copy(
            src_ref=total_ref.at[owned(me)],
            dst_ref=total_ref.at[owned(source)],
            send_sem=bs_sem.at[k],
            recv_sem=br_sem.at[k],
            device_id={"space": lax.rem(me + k, spaces)},
            device_id_type=MESH,
        ).wait_recv()
    for k in range(1, spaces):
        scatter(k).wait_send()
        spread(k).wait_send()

    def drain(c, carry):
        hop(early, c).wait_send()

        @pl.when(place(late) < snaps - 1)
        def _():
            hop(late, c).wait_send()

        return carry

    lax.fori_loop(0, count, drain, 0)


def gather(x, sel, spaces, snaps, chunk):
    rows, wide = x.shape[0], sel.shape[1]
    count = rows // chunk
    height = 5 * wide // 2
    block = -(-height // (8 * spaces)) * 8
    return pl.pallas_call(
        functools.partial(gather_kernel, spaces, snaps, chunk, block),
        out_shape=(
            jax.ShapeDtypeStruct((rows, wide), jnp.float32),
            jax.ShapeDtypeStruct((spaces * block, LANES), jnp.float32),
        ),
        in_specs=[pl.BlockSpec(memory_space=pltpu.VMEM)] * 2,
        out_specs=[pl.BlockSpec(memory_space=pltpu.VMEM)] * 2,
        scratch_shapes=[
            pltpu.VMEM((rows, wide), jnp.float32),
            pltpu.VMEM((2, rows, wide), jnp.float32),
            pltpu.VMEM((spaces * block, LANES), jnp.float32),
            pltpu.VMEM((spaces, block, LANES), jnp.float32),
            pltpu.SemaphoreType.DMA((2, count)),
            pltpu.SemaphoreType.DMA((2, count)),
            pltpu.SemaphoreType.DMA((spaces,)),
            pltpu.SemaphoreType.DMA((spaces,)),
            pltpu.SemaphoreType.DMA((spaces,)),
            pltpu.SemaphoreType.DMA((spaces,)),
        ],
        compiler_params=pltpu.CompilerParams(
            collective_id=0, has_side_effects=True, vmem_limit_bytes=40 * 2 ** 20
        ),
        name="gather_panel",
    )(x, sel)


def inverse_factor(square, out):
    size = square.shape[0]
    groups = size // 8
    left = [square[8 * g:8 * g + 8, :] for g in range(groups)]
    lane = lax.broadcasted_iota(jnp.int32, (8, size), 1)
    row = lax.broadcasted_iota(jnp.int32, (8, size), 0)
    right = [(lane == row + 8 * g).astype(jnp.float32) for g in range(groups)]
    for j in range(size):
        g, s = divmod(j, 8)
        pivot = left[g][s:s + 1, j:j + 1]
        line = left[g][s:s + 1, :] / pivot
        unit = right[g][s:s + 1, :]
        out[j:j + 1, :] = unit / jnp.sqrt(pivot)
        unit = unit / pivot
        for b in range(g, groups):
            if b == g and s == 7:
                continue
            factor = jnp.broadcast_to(left[b][:, j:j + 1], (8, size))
            if b == g:
                factor = jnp.where(row > s, factor, 0.0)
            left[b] = left[b] - factor * line
            right[b] = right[b] - factor * unit


def finish_kernel(scale, total_ref, panel_ref, x_ref, res_ref, basis_ref, inv1, inv2, inv, weights):
    @pl.when(pl.program_id(0) == 0)
    def _():
        n = LANES
        inverse_factor(total_ref[0:n, :], inv1)
        first = inv1[...]
        low = dot(total_ref[n:2 * n, :], first, ((1,), (1,)))
        rest = total_ref[4 * n:5 * n, :] - dot(low, low, ((1,), (1,)))
        inverse_factor(rest, inv2)
        second = inv2[...]
        inv[0:n, 0:n] = first
        inv[0:n, n:2 * n] = jnp.zeros((n, n), jnp.float32)
        inv[n:2 * n, 0:n] = -dot(second, dot(low, first))
        inv[n:2 * n, n:2 * n] = second
        weights[...] = dot(inv[...], total_ref[2 * n:4 * n, :])

    fresh = dot(panel_ref[...], inv[...], ((1,), (1,)))
    basis_ref[...] = fresh * scale
    res_ref[...] = x_ref[...] - dot(fresh, weights[...])


def finish(total, panel, x, scale, tile):
    rows, wide = panel.shape
    return pl.pallas_call(
        functools.partial(finish_kernel, scale),
        grid=(rows // tile,),
        out_shape=(
            jax.ShapeDtypeStruct(x.shape, jnp.float32),
            jax.ShapeDtypeStruct(panel.shape, jnp.float32),
        ),
        in_specs=[
            pl.BlockSpec(total.shape, lambda i: (0, 0)),
            pl.BlockSpec((tile, wide), lambda i: (i, 0)),
            pl.BlockSpec((tile, x.shape[1]), lambda i: (i, 0)),
        ],
        out_specs=[
            pl.BlockSpec((tile, x.shape[1]), lambda i: (i, 0)),
            pl.BlockSpec((tile, wide), lambda i: (i, 0)),
        ],
        scratch_shapes=[
            pltpu.VMEM((LANES, LANES), jnp.float32),
            pltpu.VMEM((LANES, LANES), jnp.float32),
            pltpu.VMEM((2 * LANES, 2 * LANES), jnp.float32),
            pltpu.VMEM((2 * LANES, LANES), jnp.float32),
        ],
        compiler_params=pltpu.CompilerParams(vmem_limit_bytes=24 * 2 ** 20),
        name="finish_basis",
    )(total, panel, x)


def solution(mesh):
    spaces, snaps = mesh.shape["space"], mesh.shape["snap"]

    def on_device(x, picks):
        rows, cols = x.shape
        column = jnp.arange(cols, dtype=jnp.int32) + lax.axis_index("snap") * cols
        sel = (column[:, None] == picks.reshape(1, -1)).astype(jnp.float32)
        panel, total = gather(x, sel, spaces, snaps, 256)
        return finish(total, panel, x, math.sqrt(rows * spaces), 512)

    return jax.shard_map(
        on_device,
        mesh=mesh,
        in_specs=(P("space", "snap"), P()),
        out_specs=(P("space", "snap"), P("space", None)),
        check_vma=False,
    )
```

time: 426 us -> 167 us (0.39)
  waiting for transfers between devices: 290 us -> 0 us
  Pallas kernels: 0 us -> 164 us
  matrix products: 63.7 us -> 0 us
  other arithmetic: 50.7 us -> 0.77 us
  between operations: 14.2 us -> 0.66 us
  local copies, waits for them, and re-layouts: 8.13 us -> 1.59 us
    pallas_call x0 -> x2, Pallas kernels: none -> 164 us  [the longest x1 126 us: gather(): pl.pallas_call(functools.partial(gather_kernel, spaces, snaps, chunk, blo...]
    all_gather x1 -> x0, waiting for transfers between devices: 153 us -> none  [fetch_panel(): piece = lax.all_gather(snapshots, 'snap', axis=1, tiled=True)]
    psum x3 -> x0, waiting for transfers between devices: 135 us -> none  [the longest x2 95.5 us: on_device(): weights = lax.psum(tdot(fresh, residual), 'space')]
    another operation x10 -> x0, other arithmetic: 45.7 us -> none  [the longest x6 24.8 us: on_device(): lower = jnp.linalg.cholesky(gram)]
    dot_general x11 -> x0, matrix products: 45.4 us -> none  [the longest x5 32.2 us: hdot(): jnp.dot(left, right, precision=lax.Precision.HIGHEST, preferred_element_t...]
    another operation x2 -> x0, matrix products: 18.3 us -> none  [on_device(): fresh = jax.scipy.linalg.solve_triangular(lower, panel.T, lower=True).T]
    unnamed x25 -> x2, local copies, waits for them, and re-layouts: 7.11 us -> 1.59 us
  transfers between devices with their start and end apart: 4 -> 0, of which waited for: 4 -> 0; matrix products, arithmetic and copies ran while one was open for 5% -> 0% of each run, Pallas kernels for 0% -> 0%
where the time goes in v1:
time: 167 us
  Pallas kernels  164 us (98%)
    pallas_call x1, Pallas kernels, gather(): pl.pallas_call(functools.partial(gather_kernel, spaces, snaps, chunk, blo...  126 us
    pallas_call x1, Pallas kernels, finish(): pl.pallas_call(functools.partial(finish_kernel, scale), grid=(rows // til...  37.7 us

profile of v1, /device:TPU:0, one launch (start us, length us, event | category | flops | bytes accessed | tf_op | source)
XLA Modules:
  0.0 167.0 jit_solution(5417882204160349274)
XLA Ops:
  0.6 0.8 compare_convert_fusion.sel_ref
  1.4 0.0 copy-start
  1.4 1.6 copy-done
  3.0 126.3 %gather_panel.1 = (f32[4096,256]{1,0:T(8,128)S(1)}, f32[640,128]{1,0:T(8,128)S(1)}) custom-call(f32[4096,128]{1,0:T(8,128)S(1)} %copy-done, f32[128,256]{1,0:T(8,128)S(1)} %compare_convert_fusion.sel_ref), custom_call_target="tpu_custom_call" | custom-call | tf_op jit(solution)/shard_map/gather_panel/pallas_call | solution.py:178
  129.3 37.7 %finish_basis.1 = (f32[4096,128]{1,0:T(8,128)}, f32[4096,256]{1,0:T(8,128)}) custom-call(f32[640,128]{1,0:T(8,128)S(1)} %get-tuple-element.4.total_ref, f32[4096,256]{1,0:T(8,128)S(1)} %get-tuple-element.5.panel_ref, f32[4096,128]{1,0:T(8,128)S(1)} %copy-done), custom_call_target="tpu_custom_call" | custom-call | tf_op jit(solution)/shard_map/finish_basis/pallas_call | solution.py:252
  (1 shorter events, 0.0 us)
Async XLA Ops:
  1.4 1.6 copy-start

commit v2 on v1

--- a/solution.py
+++ b/solution.py
@@ -21,7 +21,7 @@
 
 def gather_kernel(
     spaces, snaps, chunk, block,
-    x_ref, sel_ref, panel_ref, total_ref,
+    x_ref, picks_ref, panel_ref, total_ref,
     own, acc, gram, parts,
     send_sem, recv_sem, gs_sem, gr_sem, bs_sem, br_sem,
 ):
@@ -29,7 +29,9 @@
     z = lax.axis_index("snap")
     rows = x_ref.shape[0]
     count = rows // chunk
-    lag = min(2, count)
+    cols = x_ref.shape[1]
+    column = lax.broadcasted_iota(jnp.int32, (cols, picks_ref.shape[1]), 0) + z * cols
+    chosen = (column == picks_ref[...]).astype(jnp.float32)
     early = z // (snaps // 2)
     late = 1 - early
 
@@ -61,7 +63,7 @@
         )
 
     def prepare(c, carry):
-        mine = dot(x_ref[span(c), :], sel_ref[...])
+        mine = dot(x_ref[span(c), :], chosen)
         own[span(c), :] = mine
 
         @pl.when(place(early) == 0)
@@ -81,35 +83,45 @@
             acc[early, span(c), :] = acc[early, span(c), :] + own[span(c), :]
             hop(early, c).start()
 
-    def finish(c):
+    def join(c):
         hop(late, c).wait_recv()
-        panel = acc[late, span(c), :] + acc[early, span(c), :]
-        panel_ref[span(c), :] = panel
+        came = acc[late, span(c), :]
+        panel_ref[span(c), :] = came + acc[early, span(c), :]
 
         @pl.when(place(late) < snaps - 1)
         def _():
-            acc[late, span(c), :] = acc[late, span(c), :] + own[span(c), :]
+            acc[late, span(c), :] = came + own[span(c), :]
             hop(late, c).start()
 
+    def square(pair):
+        where = pl.ds(pl.multiple_of(pair * 2 * chunk, 2 * chunk), 2 * chunk)
+        panel = panel_ref[where, :]
         half = panel.shape[1] // 2
         first, second = panel[:, :half], panel[:, half:]
-        wide = jnp.concatenate([first, x_ref[span(c), :]], axis=1)
+        wide = jnp.concatenate([first, x_ref[where, :]], axis=1)
         both = dot(panel, wide, ((0,), (0,)))
         gram[0:2 * half, :] += both[:, :half]
         gram[2 * half:4 * half, :] += both[:, half:]
         gram[4 * half:5 * half, :] += dot(second, second, ((0,), (0,)))
 
-    for c in range(lag):
+    for c in range(4):
         relay(c)
-
-    def step(c, carry):
-        relay(c)
-        finish(c - lag)
+    join(0)
+
+    def step(t, carry):
+        relay(2 * t)
+        join(2 * t - 3)
+        square(t - 2)
+        relay(2 * t + 1)
+        join(2 * t - 2)
         return carry
 
-    lax.fori_loop(lag, count, step, 0)
-    for c in range(count - lag, count):
-        finish(c)
+    lax.fori_loop(2, count // 2, step, 0)
+    join(count - 3)
+    square(count // 2 - 2)
+    join(count - 2)
+    join(count - 1)
+    square(count // 2 - 1)
 
     def owned(k):
         return pl.ds(pl.multiple_of(k * block, block), block)
@@ -170,8 +182,8 @@
     lax.fori_loop(0, count, drain, 0)
 
 
-def gather(x, sel, spaces, snaps, chunk):
-    rows, wide = x.shape[0], sel.shape[1]
+def gather(x, picks, spaces, snaps, chunk):
+    rows, wide = x.shape[0], picks.shape[1]
     count = rows // chunk
     height = 5 * wide // 2
     block = -(-height // (8 * spaces)) * 8
@@ -199,7 +211,7 @@
             collective_id=0, has_side_effects=True, vmem_limit_bytes=40 * 2 ** 20
         ),
         name="gather_panel",
-    )(x, sel)
+    )(x, picks)
 
 
 def inverse_factor(square, out):
@@ -209,21 +221,28 @@
     lane = lax.broadcasted_iota(jnp.int32, (8, size), 1)
     row = lax.broadcasted_iota(jnp.int32, (8, size), 0)
     right = [(lane == row + 8 * g).astype(jnp.float32) for g in range(groups)]
-    for j in range(size):
-        g, s = divmod(j, 8)
-        pivot = left[g][s:s + 1, j:j + 1]
-        line = left[g][s:s + 1, :] / pivot
-        unit = right[g][s:s + 1, :]
-        out[j:j + 1, :] = unit / jnp.sqrt(pivot)
-        unit = unit / pivot
-        for b in range(g, groups):
-            if b == g and s == 7:
-                continue
-            factor = jnp.broadcast_to(left[b][:, j:j + 1], (8, size))
-            if b == g:
-                factor = jnp.where(row > s, factor, 0.0)
-            left[b] = left[b] - factor * line
-            right[b] = right[b] - factor * unit
+    for g in range(groups):
+        line, unit = left[g], right[g]
+        spread = [
+            jnp.broadcast_to(line[:, 8 * g + c:8 * g + c + 1], (8, size)) for c in range(8)
+        ]
+        scale = jnp.zeros((8, size), jnp.float32)
+        for s in range(8):
+            invert = 1.0 / spread[s][s:s + 1, :]
+            scale = jnp.where(row == s, invert, scale)
+            if s == 7:
+                break
+            factor = jnp.where(row > s, spread[s] * invert, 0.0)
+            for c in range(s + 1, 8):
+                spread[c] = spread[c] - factor * spread[c][s:s + 1, :]
+            line = line - factor * line[s:s + 1, :]
+            unit = unit - factor * unit[s:s + 1, :]
+        out[8 * g:8 * g + 8, :] = unit * jnp.sqrt(scale)
+        if g + 1 < groups:
+            tail = dot(line, jnp.concatenate([line * scale, unit * scale], axis=1), ((0,), (0,)))
+            for b in range(g + 1, groups):
+                left[b] = left[b] - tail[8 * b:8 * b + 8, :size]
+                right[b] = right[b] - tail[8 * b:8 * b + 8, size:]
 
 
 def finish_kernel(scale, total_ref, panel_ref, x_ref, res_ref, basis_ref, inv1, inv2, inv, weights):
@@ -280,10 +299,8 @@
     spaces, snaps = mesh.shape["space"], mesh.shape["snap"]
 
     def on_device(x, picks):
-        rows, cols = x.shape
-        column = jnp.arange(cols, dtype=jnp.int32) + lax.axis_index("snap") * cols
-        sel = (column[:, None] == picks.reshape(1, -1)).astype(jnp.float32)
-        panel, total = gather(x, sel, spaces, snaps, 256)
+        rows = x.shape[0]
+        panel, total = gather(x, picks.reshape(1, -1), spaces, snaps, 64)
         return finish(total, panel, x, math.sqrt(rows * spaces), 512)
 
     return jax.shard_map(

time: 167 us -> 163 us (0.976)
  Pallas kernels: 164 us -> 160 us
    pallas_call x1, Pallas kernels: 37.7 us -> 32.9 us  [finish(): pl.pallas_call(functools.partial(finish_kernel, scale), grid=(rows // til...]
where the time goes in v2:
time: 163 us
  Pallas kernels  160 us (98%)
  local copies, waits for them, and re-layouts  2.26 us (1%)
    pallas_call x1, Pallas kernels, gather(): pl.pallas_call(functools.partial(gather_kernel, spaces, snaps, chunk, blo...  127 us
    pallas_call x1, Pallas kernels, finish(): pl.pallas_call(functools.partial(finish_kernel, scale), grid=(rows // til...  32.9 us

profile of v2, /device:TPU:0, one launch (start us, length us, event | category | flops | bytes accessed | tf_op | source)
XLA Modules:
  0.0 162.8 jit_solution(12503906805022357887)
XLA Ops:
  0.6 0.0 copy-start
  0.6 1.6 copy-done
  2.2 0.0 copy-start.1
  2.2 0.7 copy-done.1
  2.9 127.0 %gather_panel.1 = (f32[4096,256]{1,0:T(8,128)S(1)}, f32[640,128]{1,0:T(8,128)S(1)}) custom-call(f32[4096,128]{1,0:T(8,128)S(1)} %copy-done, s32[1,256]{1,0:T(1,128)S(1)} %bitcast.1), custom_call_target="tpu_custom_call" | custom-call | tf_op jit(solution)/shard_map/gather_panel/pallas_call | solution.py:190
  129.9 32.9 %finish_basis.1 = (f32[4096,128]{1,0:T(8,128)}, f32[4096,256]{1,0:T(8,128)}) custom-call(f32[640,128]{1,0:T(8,128)S(1)} %get-tuple-element.4.total_ref, f32[4096,256]{1,0:T(8,128)S(1)} %get-tuple-element.5.panel_ref, f32[4096,128]{1,0:T(8,128)S(1)} %copy-done), custom_call_target="tpu_custom_call" | custom-call | tf_op jit(solution)/shard_map/finish_basis/pallas_call | solution.py:271
Async XLA Ops:
  0.6 1.6 copy-start
  2.2 0.7 copy-start.1

commit v3 on v2

--- a/solution.py
+++ b/solution.py
@@ -62,25 +62,25 @@
             device_id_type=MESH,
         )
 
-    def prepare(c, carry):
-        mine = dot(x_ref[span(c), :], chosen)
-        own[span(c), :] = mine
-
-        @pl.when(place(early) == 0)
-        def _():
+    @pl.when(place(early) == 0)
+    def _():
+        def prepare(c, carry):
+            mine = dot(x_ref[span(c), :], chosen)
             acc[early, span(c), :] = mine
             hop(early, c).start()
-
-        return carry
-
-    lax.fori_loop(0, count, prepare, 0)
+            return carry
+
+        lax.fori_loop(0, count, prepare, 0)
+
     gram[...] = jnp.zeros_like(gram)
 
     def relay(c):
         @pl.when(place(early) > 0)
         def _():
+            mine = dot(x_ref[span(c), :], chosen)
+            own[span(c), :] = mine
             hop(early, c).wait_recv()
-            acc[early, span(c), :] = acc[early, span(c), :] + own[span(c), :]
+            acc[early, span(c), :] = acc[early, span(c), :] + mine
             hop(early, c).start()
 
     def join(c):
@@ -245,7 +245,23 @@
                 right[b] = right[b] - tail[8 * b:8 * b + 8, size:]
 
 
-def finish_kernel(scale, total_ref, panel_ref, x_ref, res_ref, basis_ref, inv1, inv2, inv, weights):
+def split(value):
+    high = value.astype(jnp.bfloat16)
+    return high, (value - high.astype(jnp.float32)).astype(jnp.bfloat16)
+
+
+def dot3(left, high, low):
+    def part(a, b):
+        return jnp.dot(a, b, preferred_element_type=jnp.float32)
+
+    top, rest = split(left)
+    return part(top, high) + (part(top, low) + part(rest, high))
+
+
+def finish_kernel(
+    scale, total_ref, panel_ref, x_ref, res_ref, basis_ref,
+    inv1, inv2, inv, inv_high, inv_low, w_high, w_low,
+):
     @pl.when(pl.program_id(0) == 0)
     def _():
         n = LANES
@@ -259,11 +275,12 @@
         inv[0:n, n:2 * n] = jnp.zeros((n, n), jnp.float32)
         inv[n:2 * n, 0:n] = -dot(second, dot(low, first))
         inv[n:2 * n, n:2 * n] = second
-        weights[...] = dot(inv[...], total_ref[2 * n:4 * n, :])
-
-    fresh = dot(panel_ref[...], inv[...], ((1,), (1,)))
+        w_high[...], w_low[...] = split(dot(inv[...], total_ref[2 * n:4 * n, :]))
+        inv_high[...], inv_low[...] = split(inv[...].T)
+
+    fresh = dot3(panel_ref[...], inv_high[...], inv_low[...])
     basis_ref[...] = fresh * scale
-    res_ref[...] = x_ref[...] - dot(fresh, weights[...])
+    res_ref[...] = x_ref[...] - dot3(fresh, w_high[...], w_low[...])
 
 
 def finish(total, panel, x, scale, tile):
@@ -288,7 +305,10 @@
             pltpu.VMEM((LANES, LANES), jnp.float32),
             pltpu.VMEM((LANES, LANES), jnp.float32),
             pltpu.VMEM((2 * LANES, 2 * LANES), jnp.float32),
-            pltpu.VMEM((2 * LANES, LANES), jnp.float32),
+            pltpu.VMEM((2 * LANES, 2 * LANES), jnp.bfloat16),
+            pltpu.VMEM((2 * LANES, 2 * LANES), jnp.bfloat16),
+            pltpu.VMEM((2 * LANES, LANES), jnp.bfloat16),
+            pltpu.VMEM((2 * LANES, LANES), jnp.bfloat16),
         ],
         compiler_params=pltpu.CompilerParams(vmem_limit_bytes=24 * 2 ** 20),
         name="finish_basis",

time: 163 us -> 148 us (0.908)
  Pallas kernels: 160 us -> 145 us
    pallas_call x1, Pallas kernels: 127 us -> 119 us  [gather(): pl.pallas_call(functools.partial(gather_kernel, spaces, snaps, chunk, blo...]
    pallas_call x1, Pallas kernels: 32.9 us -> 26.2 us  [finish(): pl.pallas_call(functools.partial(finish_kernel, scale), grid=(rows // til...]
where the time goes in v3:
time: 148 us
  Pallas kernels  145 us (98%)
  local copies, waits for them, and re-layouts  2.26 us (2%)
    pallas_call x1, Pallas kernels, gather(): pl.pallas_call(functools.partial(gather_kernel, spaces, snaps, chunk, blo...  119 us
    pallas_call x1, Pallas kernels, finish(): pl.pallas_call(functools.partial(finish_kernel, scale), grid=(rows // til...  26.2 us

profile of v3, /device:TPU:0, one launch (start us, length us, event | category | flops | bytes accessed | tf_op | source)
XLA Modules:
  0.0 147.7 jit_solution(11076096858728525087)
XLA Ops:
  0.6 0.0 copy-start
  0.6 1.6 %copy-done = f32[4096,128]{1,0:T(8,128)S(1)} copy-done((f32[4096,128]{1,0:T(8,128)S(1)}, f32[4096,128]{1,0:T(8,128)}, u32[]{:S(2)}) %copy-start) | copy-done | bytes 2097176
  2.2 0.0 copy-start.1
  2.2 0.7 copy-done.1
  2.9 118.5 %gather_panel.1 = (f32[4096,256]{1,0:T(8,128)S(1)}, f32[640,128]{1,0:T(8,128)S(1)}) custom-call(f32[4096,128]{1,0:T(8,128)S(1)} %copy-done, s32[1,256]{1,0:T(1,128)S(1)} %bitcast.1), custom_call_target="tpu_custom_call" | custom-call | tf_op jit(solution)/shard_map/gather_panel/pallas_call | solution.py:190
  121.4 26.2 %finish_basis.1 = (f32[4096,128]{1,0:T(8,128)}, f32[4096,256]{1,0:T(8,128)}) custom-call(f32[640,128]{1,0:T(8,128)S(1)} %get-tuple-element.4.total_ref, f32[4096,256]{1,0:T(8,128)S(1)} %get-tuple-element.5.panel_ref, f32[4096,128]{1,0:T(8,128)S(1)} %copy-done), custom_call_target="tpu_custom_call" | custom-call | tf_op jit(solution)/shard_map/finish_basis/pallas_call | solution.py:288
Async XLA Ops:
  0.6 1.6 %copy-start = (f32[4096,128]{1,0:T(8,128)S(1)}, f32[4096,128]{1,0:T(8,128)}, u32[]{:S(2)}) copy-start(f32[4096,128]{1,0:T(8,128)} %x_ref.3) | copy-start | bytes 6291460
  2.2 0.7 copy-start.1

commit v4 on v3

--- a/solution.py
+++ b/solution.py
@@ -260,7 +260,7 @@
 
 def finish_kernel(
     scale, total_ref, panel_ref, x_ref, res_ref, basis_ref,
-    inv1, inv2, inv, inv_high, inv_low, w_high, w_low,
+    inv1, inv2, inv, high, low_part,
 ):
     @pl.when(pl.program_id(0) == 0)
     def _():
@@ -275,12 +275,14 @@
         inv[0:n, n:2 * n] = jnp.zeros((n, n), jnp.float32)
         inv[n:2 * n, 0:n] = -dot(second, dot(low, first))
         inv[n:2 * n, n:2 * n] = second
-        w_high[...], w_low[...] = split(dot(inv[...], total_ref[2 * n:4 * n, :]))
-        inv_high[...], inv_low[...] = split(inv[...].T)
-
-    fresh = dot3(panel_ref[...], inv_high[...], inv_low[...])
+        turned = inv[...].T
+        weights = dot(inv[...], total_ref[2 * n:4 * n, :])
+        high[...], low_part[...] = split(jnp.concatenate([turned, dot(turned, weights)], axis=1))
+
+    both = dot3(panel_ref[...], high[...], low_part[...])
+    fresh = both[:, :2 * LANES]
     basis_ref[...] = fresh * scale
-    res_ref[...] = x_ref[...] - dot3(fresh, w_high[...], w_low[...])
+    res_ref[...] = x_ref[...] - both[:, 2 * LANES:]
 
 
 def finish(total, panel, x, scale, tile):
@@ -305,10 +307,8 @@
             pltpu.VMEM((LANES, LANES), jnp.float32),
             pltpu.VMEM((LANES, LANES), jnp.float32),
             pltpu.VMEM((2 * LANES, 2 * LANES), jnp.float32),
-            pltpu.VMEM((2 * LANES, 2 * LANES), jnp.bfloat16),
-            pltpu.VMEM((2 * LANES, 2 * LANES), jnp.bfloat16),
-            pltpu.VMEM((2 * LANES, LANES), jnp.bfloat16),
-            pltpu.VMEM((2 * LANES, LANES), jnp.bfloat16),
+            pltpu.VMEM((2 * LANES, 3 * LANES), jnp.bfloat16),
+            pltpu.VMEM((2 * LANES, 3 * LANES), jnp.bfloat16),
         ],
         compiler_params=pltpu.CompilerParams(vmem_limit_bytes=24 * 2 ** 20),
         name="finish_basis",
@@ -321,7 +321,7 @@
     def on_device(x, picks):
         rows = x.shape[0]
         panel, total = gather(x, picks.reshape(1, -1), spaces, snaps, 64)
-        return finish(total, panel, x, math.sqrt(rows * spaces), 512)
+        return finish(total, panel, x, math.sqrt(rows * spaces), 1024)
 
     return jax.shard_map(
         on_device,

time: 148 us -> 145 us (0.980)
  Pallas kernels: 145 us -> 142 us
    pallas_call x1, Pallas kernels: 26.2 us -> 23.8 us  [finish(): pl.pallas_call(functools.partial(finish_kernel, scale), grid=(rows // til...]
where the time goes in v4:
time: 145 us
  Pallas kernels  142 us (98%)
  local copies, waits for them, and re-layouts  2.26 us (2%)
    pallas_call x1, Pallas kernels, gather(): pl.pallas_call(functools.partial(gather_kernel, spaces, snaps, chunk, blo...  119 us
    pallas_call x1, Pallas kernels, finish(): pl.pallas_call(functools.partial(finish_kernel, scale), grid=(rows // til...  23.8 us

profile of v4, /device:TPU:0, one launch (start us, length us, event | category | flops | bytes accessed | tf_op | source)
XLA Modules:
  0.0 145.2 jit_solution(8232943081382152470)
XLA Ops:
  0.6 0.0 copy-start
  0.6 1.6 %copy-done = f32[4096,128]{1,0:T(8,128)S(1)} copy-done((f32[4096,128]{1,0:T(8,128)S(1)}, f32[4096,128]{1,0:T(8,128)}, u32[]{:S(2)}) %copy-start) | copy-done | bytes 2097176
  2.2 0.0 copy-start.1
  2.2 0.7 copy-done.1
  2.9 118.5 %gather_panel.1 = (f32[4096,256]{1,0:T(8,128)S(1)}, f32[640,128]{1,0:T(8,128)S(1)}) custom-call(f32[4096,128]{1,0:T(8,128)S(1)} %copy-done, s32[1,256]{1,0:T(1,128)S(1)} %bitcast.1), custom_call_target="tpu_custom_call" | custom-call | tf_op jit(solution)/shard_map/gather_panel/pallas_call | solution.py:190
  121.4 23.8 %finish_basis.1 = (f32[4096,128]{1,0:T(8,128)}, f32[4096,256]{1,0:T(8,128)}) custom-call(f32[640,128]{1,0:T(8,128)S(1)} %get-tuple-element.4.total_ref, f32[4096,256]{1,0:T(8,128)S(1)} %get-tuple-element.5.panel_ref, f32[4096,128]{1,0:T(8,128)S(1)} %copy-done), custom_call_target="tpu_custom_call" | custom-call | tf_op jit(solution)/shard_map/finish_basis/pallas_call | solution.py:290
Async XLA Ops:
  0.6 1.6 %copy-start = (f32[4096,128]{1,0:T(8,128)S(1)}, f32[4096,128]{1,0:T(8,128)}, u32[]{:S(2)}) copy-start(f32[4096,128]{1,0:T(8,128)} %x_ref.3) | copy-start | bytes 6291460
  2.2 0.7 copy-start.1
